TPU v7x, 256 devices: a whole 4x4x8 slice. The times are simulated.
256 devices in a mesh: ens: 4 (over y_hi, core), grid: 64 (over x, y_lo, z).
Axes of the slice: x: 4, y: 4 (y_hi: 2, y_lo: 2; y = y_hi * 2 + y_lo), z: 8, core: 2. Of those that a mesh axis runs over, the one named last changes fastest.
Arguments:
- members: bfloat16 [8, 16384, 1024], P('ens', 'grid'), may hold values from -6 to 6
- observed_truth: float32 [16384, 100], P('grid'), may hold values from -6 to 6
- cell_measure: float32 [16384], P('grid'), may hold values from 0.25 to 12, as said below
- reach: int32 [16384], P('grid'), may hold values from 1 to 128, as said below
- w_query: bfloat16 [1024, 1024], replicated, may hold values from -0.1875 to 0.1875
- w_key: bfloat16 [1024, 1024], replicated, may hold values from -0.1875 to 0.1875
- w_value: bfloat16 [1024, 1024], replicated, may hold values from -0.1875 to 0.1875
- w_out: bfloat16 [1024, 1024], replicated, may hold values from -0.75 to 0.75
- readout_coefficients: bfloat16 [1024, 100], replicated, may hold values from -0.1875 to 0.1875
Outputs:
- loss: float32 [], replicated
- adjoint_members: bfloat16 [8, 16384, 1024], P('ens', 'grid')
Inputs may be any that keep to these rules, and one draw needn't show every extreme that they name: Each point's window reach lies between 1 and 128; in every block of 256 points some have reach 128. `cell_measure`: positive point weights.
All inputs are finite; a program needn't handle non-finite values.
Results may differ from a plain program's by a relative error of at most 0.02.
Values may be sent and summed in bfloat16 or wider, within the bound.
A program may use at most 128 MiB of HBM per device.

v0:
```python
import functools
import math

import jax
import jax.numpy as jnp
from jax import lax
from jax.experimental import pallas as pl
from jax.experimental.pallas import tpu as pltpu
from jax.sharding import PartitionSpec as P

MESH = pl.DeviceIdType.MESH
F32 = jnp.float32
BF16 = jnp.bfloat16
HEAD = 64
HALF = 128
LANES = 128
COLS = 256
WINDOW = 3 * HALF
EPS = 1e-05
SOFT2 = 0.01
SOFT = 0.1
LOG2E = math.log2(math.e)
LN2 = math.log(2.0)

NN = (((1,), (0,)), ((), ()))
NT = (((1,), (1,)), ((), ()))


def dot(a, b, dims=NN):
    return lax.dot_general(a, b, dims, preferred_element_type=F32)


def flip(index, bit):
    return index + bit * (1 - 2 * ((index // bit) % 2))


def normalise(block):
    values = block.astype(F32)
    centred = values - jnp.mean(values, axis=-1, keepdims=True)
    inverse = lax.rsqrt(jnp.mean(centred * centred, axis=-1, keepdims=True) + EPS)
    return centred * inverse, inverse


def per_head(pair):
    low = lax.broadcasted_iota(jnp.int32, pair.shape, 1) < HEAD
    zero = jnp.zeros_like(pair)
    return jnp.concatenate([jnp.where(low, pair, zero), jnp.where(low, zero, pair)], axis=0)


def own_head(wide):
    both = jnp.concatenate([wide[:HEAD, :HALF], wide[HEAD:, HALF:]], axis=0)
    return both.T


def kernel(
    ens_size,
    grid_size,
    nvars,
    members,
    truth_in,
    measure_in,
    reach_in,
    w_query,
    w_key,
    w_value,
    w_out,
    readout_in,
    loss_out,
    out,
    mem,
    halo,
    wq,
    wk,
    wv,
    wo,
    readout,
    truth,
    measure,
    bias,
    normed_own,
    normed_halo,
    q_s,
    k_s,
    v_s,
    p_s,
    attended,
    forecasts,
    adj_mixed,
    adj_mixed_b,
    adj_attended,
    dq_s,
    dk_s,
    dv_s,
    rim_k,
    rim_v,
    rim_out,
    rim_in,
    adj_normed,
    loss_acc,
    loss_in,
    load_sem,
    halo_send,
    halo_recv,
    ens_send,
    ens_recv,
    rim_send,
    rim_recv,
    loss_send,
    loss_recv,
):
    count, rows, width = members.shape
    pairs = width // LANES
    chunks = width // COLS
    tiles = rows // HALF
    ens = lax.axis_index("ens")
    grid = lax.axis_index("grid")
    right = lax.rem(grid + 1, grid_size)
    left = lax.rem(grid + grid_size - 1, grid_size)
    first = grid * rows
    total_points = rows * grid_size
    ens_partners = [{"ens": flip(ens, 1)}, {"ens": flip(ens, 2)}, {"ens": flip(flip(ens, 1), 2)}]
    ens_partners = ens_partners[: ens_size - 1]
    rounds = [{"ens": flip(ens, 1 << b)} for b in range(ens_size.bit_length() - 1)]
    rounds += [{"grid": flip(grid, 1 << b)} for b in range(grid_size.bit_length() - 1)]

    def remote(source, target, send, recv, device):
        return pltpu.make_async_remote_copy(
            src_ref=source,
            dst_ref=target,
            send_sem=send,
            recv_sem=recv,
            device_id=device,
            device_id_type=MESH,
        )

    loads = []
    for m in range(count):
        loads.append(pltpu.make_async_copy(members.at[m], mem.at[m], load_sem.at[m]))
    for n, (source, target) in enumerate(((w_query, wq), (w_key, wk), (w_value, wv), (w_out, wo))):
        loads.append(pltpu.make_async_copy(source, target, load_sem.at[count + n]))
    for load in loads:
        load.start()

    barrier = pltpu.get_barrier_semaphore()
    greeted = [{"grid": left}, {"grid": right}] + ens_partners + rounds
    for device in greeted:
        pl.semaphore_signal(barrier, inc=1, device_id=device, device_id_type=MESH)
    pl.semaphore_wait(barrier, len(greeted))

    halo_copies = []
    for m in range(count):
        to_left = remote(
            members.at[m, pl.ds(0, HALF)],
            halo.at[m, pl.ds(HALF, HALF)],
            halo_send.at[m, 0],
            halo_recv.at[m, 0],
            {"grid": left},
        )
        to_right = remote(
            members.at[m, pl.ds(rows - HALF, HALF)],
            halo.at[m, pl.ds(0, HALF)],
            halo_send.at[m, 1],
            halo_recv.at[m, 1],
            {"grid": right},
        )
        to_left.start()
        to_right.start()
        halo_copies.append((to_left, to_right))

    readout[...] = jnp.zeros_like(readout)
    readout[:, :nvars] = readout_in[...]
    truth[...] = jnp.zeros_like(truth)
    truth[:, :nvars] = truth_in[...]
    for t in range(tiles):
        part = pl.ds(t * HALF, HALF)
        row = jnp.broadcast_to(measure_in[:, t * HALF : (t + 1) * HALF], (HALF, HALF))
        measure[part, :] = row.T
        offset = lax.broadcasted_iota(jnp.int32, (WINDOW, HALF), 0) - HALF
        query = lax.broadcasted_iota(jnp.int32, (WINDOW, HALF), 1)
        point = offset + (first + t * HALF)
        reach = reach_in[:, t * HALF : (t + 1) * HALF]
        inside = (jnp.abs(offset - query) <= reach) & (point >= 0) & (point < total_points)
        bias[t] = jnp.where(inside, 0.0, -1e30).astype(F32)

    for m in range(count):
        loads[m].wait()
        for t in range(tiles):
            normed, _ = normalise(mem[m, t * HALF : (t + 1) * HALF])
            normed_own[pl.ds(m * rows + t * HALF, HALF), :] = normed.astype(BF16)
    for n in range(4):
        loads[count + n].wait()

    def project_own(c, carry):
        columns = pl.ds(pl.multiple_of(c * COLS, COLS), COLS)
        left_side = normed_own[...]
        query = (dot(left_side, wq[:, columns]) * (HEAD**-0.5 * LOG2E)).astype(BF16)
        for m in range(count):
            for j in range(2):
                q_s[m, 2 * c + j] = query[m * rows : (m + 1) * rows, j * LANES : (j + 1) * LANES]
        for weight, target in ((wk, k_s), (wv, v_s)):
            result = dot(left_side, weight[:, columns]).astype(BF16)
            for m in range(count):
                for j in range(2):
                    target[m, 2 * c + j, pl.ds(HALF, rows), :] = result[
                        m * rows : (m + 1) * rows, j * LANES : (j + 1) * LANES
                    ]
        return carry

    lax.fori_loop(0, chunks, project_own, 0)

    def attend(m, p, carry):
        keys = k_s[m, p]
        values_t = v_s[m, p].T
        for t in range(tiles):
            query = per_head(q_s[m, p, t * HALF : (t + 1) * HALF])
            window = slice(t * HALF, t * HALF + WINDOW)
            scores = dot(keys[window], query, NT)
            scores = scores + jnp.concatenate([bias[t]] * 2, axis=1)
            top = jnp.max(scores, axis=0, keepdims=True)
            weights = jnp.exp2(scores - top)
            weights = weights * (1.0 / jnp.sum(weights, axis=0, keepdims=True))
            weights = weights.astype(BF16)
            p_s[m, t, p] = weights
            blended = own_head(dot(values_t[:, window], weights))
            attended[
                pl.ds(m * rows + t * HALF, HALF), pl.ds(pl.multiple_of(p * LANES, LANES), LANES)
            ] = blended.astype(BF16)
        return carry

    ens_copies = []
    for m in range(count):
        for copy in halo_copies[m]:
            copy.wait()
        for t in range(2):
            part = pl.ds(t * HALF, HALF)
            normed, _ = normalise(halo[m, part])
            normed_halo[part, :] = normed.astype(BF16)

        def project_halo(c, carry, m=m):
            columns = pl.ds(pl.multiple_of(c * COLS, COLS), COLS)
            for weight, target in ((wk, k_s), (wv, v_s)):
                result = dot(normed_halo[...], weight[:, columns]).astype(BF16)
                for j in range(2):
                    lanes = slice(j * LANES, (j + 1) * LANES)
                    target[m, 2 * c + j, pl.ds(0, HALF), :] = result[:HALF, lanes]
                    target[m, 2 * c + j, pl.ds(HALF + rows, HALF), :] = result[HALF:, lanes]
            return carry

        lax.fori_loop(0, chunks, project_halo, 0)
        lax.fori_loop(0, pairs, functools.partial(attend, m), 0)

        def mix(c, total, m=m):
            columns = pl.ds(pl.multiple_of(c * COLS, COLS), COLS)
            mixed = dot(attended[pl.ds(m * rows, rows), :], wo[:, columns])
            mixed = mixed + mem[m, :, columns].astype(F32)
            return total + dot(mixed.astype(BF16), readout[columns, :])

        forecasts[0, m] = lax.fori_loop(0, chunks, mix, jnp.zeros((rows, LANES), F32))
        for slot, device in enumerate(ens_partners):
            copy = remote(
                forecasts.at[0, m],
                forecasts.at[slot + 1, m],
                ens_send.at[slot, m],
                ens_recv.at[slot, m],
                device,
            )
            copy.start()
            ens_copies.append(copy)

    for copy in ens_copies:
        copy.wait()

    realizations = count * ens_size
    factor = 1.0 / (realizations - 1)
    real = lax.broadcasted_iota(jnp.int32, (HALF, LANES), 1) < nvars
    score = jnp.zeros((HALF, LANES), F32)
    for t in range(tiles):
        part = slice(t * HALF, (t + 1) * HALF)
        weight = measure[part, :]
        for m in range(count):
            mine = forecasts[0, m, part]
            pair_sum = jnp.zeros((HALF, LANES), F32)
            pair_slope = jnp.zeros((HALF, LANES), F32)
            for slot in range(ens_size):
                for other in range(count):
                    if slot == 0 and other == m:
                        continue
                    gap = mine - forecasts[slot, other, part]
                    square = gap * gap + SOFT2
                    root = lax.rsqrt(square)
                    pair_sum = pair_sum + square * root
                    pair_slope = pair_slope + gap * root
            gap = mine - truth[part, :]
            square = gap * gap + SOFT2
            root = lax.rsqrt(square)
            score = score + weight * (square * root - 0.5 * factor * pair_sum)
            slope = weight * (gap * root - factor * pair_slope)
            adj_mixed_b[pl.ds(m * rows + t * HALF, HALF), pl.ds(0, LANES)] = slope.astype(BF16)
    score = jnp.where(real, score, 0.0)
    loss_acc[0] = jnp.broadcast_to(jnp.sum(score, keepdims=True), (8, LANES))

    pending = []

    def loss_step(stage):
        if stage > 0 and stage <= len(rounds):
            pending[stage - 1].wait()
            loss_acc[stage] = loss_acc[stage - 1] + loss_in[stage - 1]
        if stage < len(rounds):
            copy = remote(
                loss_acc.at[stage],
                loss_in.at[stage],
                loss_send.at[stage],
                loss_recv.at[stage],
                rounds[stage],
            )
            copy.start()
            pending.append(copy)

    loss_step(0)

    slopes = adj_mixed_b[:, :LANES]

    def spread(c, carry):
        columns = pl.ds(pl.multiple_of(c * COLS, COLS), COLS)
        adj_mixed[:, columns] = dot(slopes, readout[columns, :], NT)
        return carry

    lax.fori_loop(0, chunks, spread, 0)
    adj_mixed_b[...] = adj_mixed[...].astype(BF16)

    def back_out(c, carry):
        columns = pl.ds(pl.multiple_of(c * COLS, COLS), COLS)
        adj_attended[:, columns] = dot(adj_mixed_b[...], wo[columns, :], NT).astype(BF16)
        return carry

    lax.fori_loop(0, chunks, back_out, 0)
    loss_step(1)

    def attend_back(m, p, carry):
        keys = k_s[m, p]
        keys_t = keys.T
        values = v_s[m, p]
        lanes = pl.ds(pl.multiple_of(p * LANES, LANES), LANES)
        key_terms = []
        value_terms = []
        for t in range(tiles):
            mine = pl.ds(m * rows + t * HALF, HALF)
            window = slice(t * HALF, t * HALF + WINDOW)
            query = per_head(q_s[m, p, t * HALF : (t + 1) * HALF])
            adjoint = per_head(adj_attended[mine, lanes])
            weights = p_s[m, t, p]
            wide = weights.astype(F32)
            adj_prob = dot(values[window], adjoint, NT)
            shift = jnp.sum(wide * adj_prob, axis=0, keepdims=True)
            adj_score = (wide * (adj_prob - shift)).astype(BF16)
            adj_query = own_head(dot(keys_t[:, window], adj_score)) * HEAD**-0.5
            dq_s[mine, lanes] = adj_query.astype(BF16)
            key_terms.append(dot(adj_score, query) * LN2)
            value_terms.append(dot(weights, adjoint))
        for terms, own, rim in ((key_terms, dk_s, rim_k), (value_terms, dv_s, rim_v)):
            low, high = terms
            rim[pl.ds(0, HALF), lanes] = low[:HALF].astype(BF16)
            rim[pl.ds(HALF, HALF), lanes] = high[2 * HALF :].astype(BF16)
            own[pl.ds(m * rows, rows), lanes] = (low[HALF:] + high[: 2 * HALF]).astype(BF16)
        return carry

    rim_copies = []
    for m in range(count):
        lax.fori_loop(0, pairs // 2, functools.partial(attend_back, m), 0)
        loss_step(2 + 3 * m)
        lax.fori_loop(pairs // 2, pairs, functools.partial(attend_back, m), 0)
        loss_step(3 + 3 * m)

        def project_rim(c, carry, m=m):
            columns = pl.ds(pl.multiple_of(c * COLS, COLS), COLS)
            term = dot(rim_k[...], wk[columns, :], NT) + dot(rim_v[...], wv[columns, :], NT)
            rim_out[m, :, columns] = term.astype(BF16)
            return carry

        lax.fori_loop(0, chunks, project_rim, 0)
        to_left = remote(
            rim_out.at[m, pl.ds(0, HALF)],
            rim_in.at[m, pl.ds(HALF, HALF)],
            rim_send.at[m, 0],
            rim_recv.at[m, 0],
            {"grid": left},
        )
        to_right = remote(
            rim_out.at[m, pl.ds(HALF, HALF)],
            rim_in.at[m, pl.ds(0, HALF)],
            rim_send.at[m, 1],
            rim_recv.at[m, 1],
            {"grid": right},
        )
        to_left.start()
        to_right.start()
        rim_copies.append((to_left, to_right))
        loss_step(4 + 3 * m)

    def back_own(c, carry):
        columns = pl.ds(pl.multiple_of(c * COLS, COLS), COLS)
        adj_normed[:, columns] = (
            dot(dq_s[...], wq[columns, :], NT)
            + dot(dk_s[...], wk[columns, :], NT)
            + dot(dv_s[...], wv[columns, :], NT)
        )
        return carry

    lax.fori_loop(0, chunks, back_own, 0)
    for stage in range(8, len(rounds) + 1):
        loss_step(stage)
    loss_out[...] = loss_acc[len(rounds), 0:1, 0:1] * (1.0 / (realizations * total_points * nvars))

    for m in range(count):
        for copy in rim_copies[m]:
            copy.wait()
        for t in range(tiles):
            part = slice(t * HALF, (t + 1) * HALF)
            mine = pl.ds(m * rows + t * HALF, HALF)
            normed, inverse = normalise(mem[m, part])
            adjoint = adj_normed[mine, :] + rim_in[m, part].astype(F32)
            adjoint = inverse * (
                adjoint
                - jnp.mean(adjoint, axis=-1, keepdims=True)
                - normed * jnp.mean(adjoint * normed, axis=-1, keepdims=True)
            )
            out[m, part] = (adj_mixed[mine, :] + adjoint).astype(BF16)


def per_device(
    ens_size,
    grid_size,
    members,
    observed_truth,
    cell_measure,
    reach,
    w_query,
    w_key,
    w_value,
    w_out,
    readout_coefficients,
):
    count, rows, width = members.shape
    nvars = observed_truth.shape[1]
    pairs = width // LANES
    tiles = rows // HALF
    all_rows = count * rows
    stages = ens_size.bit_length() + grid_size.bit_length() - 2
    vmem = pl.BlockSpec(memory_space=pltpu.VMEM)
    anywhere = pl.BlockSpec(memory_space=pl.ANY)
    dma = pltpu.SemaphoreType.DMA
    loss, adjoint = pl.pallas_call(
        functools.partial(kernel, ens_size, grid_size, nvars),
        out_shape=(
            jax.ShapeDtypeStruct((1, 1), F32),
            jax.ShapeDtypeStruct(members.shape, BF16),
        ),
        in_specs=[anywhere, vmem, vmem, vmem, anywhere, anywhere, anywhere, anywhere, vmem],
        out_specs=(vmem, vmem),
        scratch_shapes=[
            pltpu.VMEM((count, rows, width), BF16),
            pltpu.VMEM((count, 2 * HALF, width), BF16),
            pltpu.VMEM((width, width), BF16),
            pltpu.VMEM((width, width), BF16),
            pltpu.VMEM((width, width), BF16),
            pltpu.VMEM((width, width), BF16),
            pltpu.VMEM((width, LANES), BF16),
            pltpu.VMEM((rows, LANES), F32),
            pltpu.VMEM((rows, LANES), F32),
            pltpu.VMEM((tiles, WINDOW, HALF), F32),
            pltpu.VMEM((all_rows, width), BF16),
            pltpu.VMEM((2 * HALF, width), BF16),
            pltpu.VMEM((count, pairs, rows, LANES), BF16),
            pltpu.VMEM((count, pairs, rows + 2 * HALF, LANES), BF16),
            pltpu.VMEM((count, pairs, rows + 2 * HALF, LANES), BF16),
            pltpu.VMEM((count, tiles, pairs, WINDOW, 2 * HALF), BF16),
            pltpu.VMEM((all_rows, width), BF16),
            pltpu.VMEM((ens_size, count, rows, LANES), F32),
            pltpu.VMEM((all_rows, width), F32),
            pltpu.VMEM((all_rows, width), BF16),
            pltpu.VMEM((all_rows, width), BF16),
            pltpu.VMEM((all_rows, width), BF16),
            pltpu.VMEM((all_rows, width), BF16),
            pltpu.VMEM((all_rows, width), BF16),
            pltpu.VMEM((2 * HALF, width), BF16),
            pltpu.VMEM((2 * HALF, width), BF16),
            pltpu.VMEM((count, 2 * HALF, width), BF16),
            pltpu.VMEM((count, 2 * HALF, width), BF16),
            pltpu.VMEM((all_rows, width), F32),
            pltpu.VMEM((stages + 1, 8, LANES), F32),
            pltpu.VMEM((stages, 8, LANES), F32),
            dma((count + 4,)),
            dma((count, 2)),
            dma((count, 2)),
            dma((ens_size - 1, count)),
            dma((ens_size - 1, count)),
            dma((count, 2)),
            dma((count, 2)),
            dma((stages,)),
            dma((stages,)),
        ],
        compiler_params=pltpu.CompilerParams(
            collective_id=0, has_side_effects=True, vmem_limit_bytes=60 * 1024 * 1024
        ),
        cost_estimate=pl.CostEstimate(
            flops=15_000_000_000, bytes_accessed=12_000_000, transcendentals=4_000_000
        ),
    )(
        members,
        observed_truth,
        cell_measure.reshape(1, rows),
        reach.reshape(1, rows),
        w_query,
        w_key,
        w_value,
        w_out,
        readout_coefficients,
    )
    return loss[0, 0], adjoint


def solution(mesh):
    return jax.shard_map(
        functools.partial(per_device, mesh.shape["ens"], mesh.shape["grid"]),
        mesh=mesh,
        in_specs=(
            P("ens", "grid", None),
            P("grid", None),
            P("grid"),
            P("grid"),
            P(),
            P(),
            P(),
            P(),
            P(),
        ),
        out_specs=(P(), P("ens", "grid", None)),
        check_vma=False,
    )
```

profile of v0, /device:TPU:1, one launch (start us, length us, event | category | flops | bytes accessed | tf_op | source)
XLA Modules:
  0.0 101.9 jit_solution(15598386127447177250)
XLA Ops:
  0.6 1.6 %copy.11.truth_in = f32[256,100]{1,0:T(8,128)} copy(f32[256,100]{0,1:T(8,128)} %param.10) | data formatting | bytes 204800 | tf_op args[1]
  2.3 1.8 %copy.12.readout_in = bf16[1024,100]{1,0:T(8,128)(2,1)} copy(bf16[1024,100]{0,1:T(8,128)(2,1)} %param.17) | data formatting | bytes 409600 | tf_op args[8]
  4.1 93.8 %shard_map.104 = (f32[1,1]{1,0:T(1,128)}, bf16[2,256,1024]{2,1,0:T(8,128)(2,1)}) custom-call(bf16[2,256,1024]{2,1,0:T(8,128)(2,1)} %members.1, f32[256,100]{1,0:T(8,128)} %copy.11.truth_in, f32[1,256]{1,0:T(1,128)} %bitcast.3, s32[1,256]{1,0:T(1,128)} %bitcast.4, bf16[1024,1024]{1,0:T(8,128)(2,1)} %w_query.1, bf16[1024,1024]{1,0:T(8,128)(2,1)} %w_key.1, ...), custom_call_target="tpu_custom_call" | custom-call | flops 15000000512 | bytes 12000000 | tf_op jit(solution)/shard_map/pallas_call | solution.py:452
  98.5 2.3 %copy.16 = bf16[2,256,1024]{2,1,0:T(8,128)(2,1)} copy(bf16[2,256,1024]{2,1,0:T(8,128)(2,1)} %get-tuple-element.9) | data formatting | bytes 2097152
where the time goes:
time: 102 us
  Pallas kernels  93.8 us (92%)
  local copies, waits for them, and re-layouts  5.7 us (6%)
  between operations  2.39 us (2%)
    pallas_call x1, Pallas kernels, per_device(): pl.pallas_call(functools.partial(kernel, ens_size, grid_size, nvars), out...  93.8 us
    unnamed x3, local copies, waits for them, and re-layouts  5.7 us

commit v1 on v0

--- a/solution.py
+++ b/solution.py
@@ -45,6 +45,11 @@
     low = lax.broadcasted_iota(jnp.int32, pair.shape, 1) < HEAD
     zero = jnp.zeros_like(pair)
     return jnp.concatenate([jnp.where(low, pair, zero), jnp.where(low, zero, pair)], axis=0)
+
+
+def own_lanes(tall):
+    low = lax.broadcasted_iota(jnp.int32, (HALF, LANES), 1) < HEAD
+    return jnp.where(low, tall[:HALF], tall[HALF:])
 
 
 def own_head(wide):
@@ -74,6 +79,7 @@
     wv,
     wo,
     readout,
+    truth_t,
     truth,
     measure,
     bias,
@@ -85,6 +91,7 @@
     p_s,
     attended,
     forecasts,
+    shared,
     adj_mixed,
     adj_mixed_b,
     adj_attended,
@@ -167,12 +174,14 @@
         to_right.start()
         halo_copies.append((to_left, to_right))
 
-    readout[...] = jnp.zeros_like(readout)
-    readout[:, :nvars] = readout_in[...]
-    truth[...] = jnp.zeros_like(truth)
-    truth[:, :nvars] = truth_in[...]
+    adj_normed[:LANES, :] = jnp.zeros((LANES, width), F32)
+    adj_normed[:nvars, :] = readout_in[...].astype(F32)
+    readout[...] = adj_normed[:LANES, :].astype(BF16)
+    truth_t[...] = jnp.zeros_like(truth_t)
+    truth_t[:nvars, :] = truth_in[...]
     for t in range(tiles):
         part = pl.ds(t * HALF, HALF)
+        truth[part, :] = truth_t[:, t * HALF : (t + 1) * HALF].T
         row = jnp.broadcast_to(measure_in[:, t * HALF : (t + 1) * HALF], (HALF, HALF))
         measure[part, :] = row.T
         offset = lax.broadcasted_iota(jnp.int32, (WINDOW, HALF), 0) - HALF
@@ -182,36 +191,42 @@
         inside = (jnp.abs(offset - query) <= reach) & (point >= 0) & (point < total_points)
         bias[t] = jnp.where(inside, 0.0, -1e30).astype(F32)
 
+    def place(m, t):
+        return pl.ds((t * count + m) * HALF, HALF)
+
     for m in range(count):
         loads[m].wait()
         for t in range(tiles):
             normed, _ = normalise(mem[m, t * HALF : (t + 1) * HALF])
-            normed_own[pl.ds(m * rows + t * HALF, HALF), :] = normed.astype(BF16)
-    for n in range(4):
-        loads[count + n].wait()
-
-    def project_own(c, carry):
+            normed_own[place(m, t), :] = normed.astype(BF16)
+
+    def project_own(weight, target, start, factor, c, carry):
         columns = pl.ds(pl.multiple_of(c * COLS, COLS), COLS)
-        left_side = normed_own[...]
-        query = (dot(left_side, wq[:, columns]) * (HEAD**-0.5 * LOG2E)).astype(BF16)
+        result = dot(normed_own[...], weight[:, columns])
+        if factor is not None:
+            result = result * factor
+        result = result.astype(BF16)
         for m in range(count):
-            for j in range(2):
-                q_s[m, 2 * c + j] = query[m * rows : (m + 1) * rows, j * LANES : (j + 1) * LANES]
-        for weight, target in ((wk, k_s), (wv, v_s)):
-            result = dot(left_side, weight[:, columns]).astype(BF16)
-            for m in range(count):
+            for t in range(tiles):
+                first_row = (t * count + m) * HALF
                 for j in range(2):
-                    target[m, 2 * c + j, pl.ds(HALF, rows), :] = result[
-                        m * rows : (m + 1) * rows, j * LANES : (j + 1) * LANES
+                    target[m, 2 * c + j, pl.ds(start + t * HALF, HALF), :] = result[
+                        first_row : first_row + HALF, j * LANES : (j + 1) * LANES
                     ]
         return carry
 
-    lax.fori_loop(0, chunks, project_own, 0)
-
-    def attend(m, p, carry):
+    loads[count].wait()
+    own = ((wq, q_s, 0, HEAD**-0.5 * LOG2E), (wk, k_s, HALF, None), (wv, v_s, HALF, None))
+    for n, job in enumerate(own):
+        if n:
+            loads[count + n].wait()
+        lax.fori_loop(0, chunks, functools.partial(project_own, *job), 0, unroll=True)
+    loads[count + 3].wait()
+
+    def attend(m, some_tiles, p, carry):
         keys = k_s[m, p]
-        values_t = v_s[m, p].T
-        for t in range(tiles):
+        values = v_s[m, p]
+        for t in some_tiles:
             query = per_head(q_s[m, p, t * HALF : (t + 1) * HALF])
             window = slice(t * HALF, t * HALF + WINDOW)
             scores = dot(keys[window], query, NT)
@@ -221,14 +236,15 @@
             weights = weights * (1.0 / jnp.sum(weights, axis=0, keepdims=True))
             weights = weights.astype(BF16)
             p_s[m, t, p] = weights
-            blended = own_head(dot(values_t[:, window], weights))
-            attended[
-                pl.ds(m * rows + t * HALF, HALF), pl.ds(pl.multiple_of(p * LANES, LANES), LANES)
-            ] = blended.astype(BF16)
+            blended = own_lanes(dot(weights.T, values[window]))
+            lanes = pl.ds(pl.multiple_of(p * LANES, LANES), LANES)
+            attended[place(m, t), lanes] = blended.astype(BF16)
         return carry
 
-    ens_copies = []
-    for m in range(count):
+    def attend_all(m, some_tiles):
+        lax.fori_loop(0, pairs, functools.partial(attend, m, some_tiles), 0, unroll=True)
+
+    def keys_of_halo(m):
         for copy in halo_copies[m]:
             copy.wait()
         for t in range(2):
@@ -236,7 +252,7 @@
             normed, _ = normalise(halo[m, part])
             normed_halo[part, :] = normed.astype(BF16)
 
-        def project_halo(c, carry, m=m):
+        def project_halo(c, carry):
             columns = pl.ds(pl.multiple_of(c * COLS, COLS), COLS)
             for weight, target in ((wk, k_s), (wv, v_s)):
                 result = dot(normed_halo[...], weight[:, columns]).astype(BF16)
@@ -246,46 +262,65 @@
                     target[m, 2 * c + j, pl.ds(HALF + rows, HALF), :] = result[HALF:, lanes]
             return carry
 
-        lax.fori_loop(0, chunks, project_halo, 0)
-        lax.fori_loop(0, pairs, functools.partial(attend, m), 0)
-
-        def mix(c, total, m=m):
+        lax.fori_loop(0, chunks, project_halo, 0, unroll=True)
+
+    ens_copies = []
+
+    def forecast(t):
+        these = pl.ds(t * count * HALF, count * HALF)
+
+        def mix(c, total):
             columns = pl.ds(pl.multiple_of(c * COLS, COLS), COLS)
-            mixed = dot(attended[pl.ds(m * rows, rows), :], wo[:, columns])
-            mixed = mixed + mem[m, :, columns].astype(F32)
-            return total + dot(mixed.astype(BF16), readout[columns, :])
-
-        forecasts[0, m] = lax.fori_loop(0, chunks, mix, jnp.zeros((rows, LANES), F32))
+            own = [mem[m, t * HALF : (t + 1) * HALF, columns] for m in range(count)]
+            mixed = dot(attended[these, :], wo[:, columns])
+            mixed = mixed + jnp.concatenate(own, axis=0).astype(F32)
+            return total + dot(mixed.astype(BF16), readout[:, columns], NT)
+
+        zero = jnp.zeros((count * HALF, LANES), F32)
+        result = lax.fori_loop(0, chunks, mix, zero, unroll=True)
+        forecasts[t] = result
+        shared[0, t] = result.astype(BF16)
         for slot, device in enumerate(ens_partners):
             copy = remote(
-                forecasts.at[0, m],
-                forecasts.at[slot + 1, m],
-                ens_send.at[slot, m],
-                ens_recv.at[slot, m],
+                shared.at[0, t],
+                shared.at[slot + 1, t],
+                ens_send.at[slot, t],
+                ens_recv.at[slot, t],
                 device,
             )
             copy.start()
             ens_copies.append(copy)
 
-    for copy in ens_copies:
-        copy.wait()
+    for m in range(count - 1):
+        keys_of_halo(m)
+        attend_all(m, range(tiles))
+    keys_of_halo(count - 1)
+    for t in range(tiles):
+        attend_all(count - 1, (t,))
+        forecast(t)
 
     realizations = count * ens_size
     factor = 1.0 / (realizations - 1)
     real = lax.broadcasted_iota(jnp.int32, (HALF, LANES), 1) < nvars
-    score = jnp.zeros((HALF, LANES), F32)
-    for t in range(tiles):
+
+    def slopes_of(t):
         part = slice(t * HALF, (t + 1) * HALF)
         weight = measure[part, :]
+        score = jnp.zeros((HALF, LANES), F32)
+        slopes = []
         for m in range(count):
-            mine = forecasts[0, m, part]
+            mine = forecasts[t, m * HALF : (m + 1) * HALF]
             pair_sum = jnp.zeros((HALF, LANES), F32)
             pair_slope = jnp.zeros((HALF, LANES), F32)
             for slot in range(ens_size):
                 for other in range(count):
+                    theirs = slice(other * HALF, (other + 1) * HALF)
                     if slot == 0 and other == m:
                         continue
-                    gap = mine - forecasts[slot, other, part]
+                    if slot == 0:
+                        gap = mine - forecasts[t, theirs]
+                    else:
+                        gap = mine - shared[slot, t, theirs].astype(F32)
                     square = gap * gap + SOFT2
                     root = lax.rsqrt(square)
                     pair_sum = pair_sum + square * root
@@ -294,9 +329,35 @@
             square = gap * gap + SOFT2
             root = lax.rsqrt(square)
             score = score + weight * (square * root - 0.5 * factor * pair_sum)
-            slope = weight * (gap * root - factor * pair_slope)
-            adj_mixed_b[pl.ds(m * rows + t * HALF, HALF), pl.ds(0, LANES)] = slope.astype(BF16)
-    score = jnp.where(real, score, 0.0)
+            slopes.append((weight * (gap * root - factor * pair_slope)).astype(BF16))
+        return jnp.where(real, score, 0.0), jnp.concatenate(slopes, axis=0)
+
+    def back_to_attended(t, slopes):
+        these = pl.ds(t * count * HALF, count * HALF)
+
+        def spread(c, carry):
+            columns = pl.ds(pl.multiple_of(c * COLS, COLS), COLS)
+            result = dot(slopes, readout[:, columns])
+            adj_mixed[these, columns] = result
+            adj_mixed_b[these, columns] = result.astype(BF16)
+            return carry
+
+        def back_out(c, carry):
+            columns = pl.ds(pl.multiple_of(c * COLS, COLS), COLS)
+            result = dot(adj_mixed_b[these, :], wo[columns, :], NT)
+            adj_attended[these, columns] = result.astype(BF16)
+            return carry
+
+        lax.fori_loop(0, chunks, spread, 0, unroll=True)
+        lax.fori_loop(0, chunks, back_out, 0, unroll=True)
+
+    score = jnp.zeros((HALF, LANES), F32)
+    for t in range(tiles):
+        for copy in ens_copies[t * (ens_size - 1) : (t + 1) * (ens_size - 1)]:
+            copy.wait()
+        scores, slopes = slopes_of(t)
+        score = score + scores
+        back_to_attended(t, slopes)
     loss_acc[0] = jnp.broadcast_to(jnp.sum(score, keepdims=True), (8, LANES))
 
     pending = []
@@ -318,24 +379,6 @@
 
     loss_step(0)
 
-    slopes = adj_mixed_b[:, :LANES]
-
-    def spread(c, carry):
-        columns = pl.ds(pl.multiple_of(c * COLS, COLS), COLS)
-        adj_mixed[:, columns] = dot(slopes, readout[columns, :], NT)
-        return carry
-
-    lax.fori_loop(0, chunks, spread, 0)
-    adj_mixed_b[...] = adj_mixed[...].astype(BF16)
-
-    def back_out(c, carry):
-        columns = pl.ds(pl.multiple_of(c * COLS, COLS), COLS)
-        adj_attended[:, columns] = dot(adj_mixed_b[...], wo[columns, :], NT).astype(BF16)
-        return carry
-
-    lax.fori_loop(0, chunks, back_out, 0)
-    loss_step(1)
-
     def attend_back(m, p, carry):
         keys = k_s[m, p]
         keys_t = keys.T
@@ -344,7 +387,7 @@
         key_terms = []
         value_terms = []
         for t in range(tiles):
-            mine = pl.ds(m * rows + t * HALF, HALF)
+            mine = place(m, t)
             window = slice(t * HALF, t * HALF + WINDOW)
             query = per_head(q_s[m, p, t * HALF : (t + 1) * HALF])
             adjoint = per_head(adj_attended[mine, lanes])
@@ -361,41 +404,33 @@
             low, high = terms
             rim[pl.ds(0, HALF), lanes] = low[:HALF].astype(BF16)
             rim[pl.ds(HALF, HALF), lanes] = high[2 * HALF :].astype(BF16)
-            own[pl.ds(m * rows, rows), lanes] = (low[HALF:] + high[: 2 * HALF]).astype(BF16)
+            both = (low[HALF:] + high[: 2 * HALF]).astype(BF16)
+            for t in range(tiles):
+                own[place(m, t), lanes] = both[t * HALF : (t + 1) * HALF]
         return carry
 
-    rim_copies = []
+    rim_copies = [[] for _ in range(count)]
     for m in range(count):
-        lax.fori_loop(0, pairs // 2, functools.partial(attend_back, m), 0)
+        lax.fori_loop(0, pairs // 2, functools.partial(attend_back, m), 0, unroll=True)
+        loss_step(1 + 3 * m)
+        lax.fori_loop(pairs // 2, pairs, functools.partial(attend_back, m), 0, unroll=True)
         loss_step(2 + 3 * m)
-        lax.fori_loop(pairs // 2, pairs, functools.partial(attend_back, m), 0)
+
+        for c in range(chunks):
+            columns = slice(c * COLS, (c + 1) * COLS)
+            term = dot(rim_k[...], wk[columns, :], NT) + dot(rim_v[...], wv[columns, :], NT)
+            rim_out[m, c] = term.astype(BF16)
+            for side, device in enumerate((left, right)):
+                copy = remote(
+                    rim_out.at[m, c, pl.ds(side * HALF, HALF)],
+                    rim_in.at[m, c, pl.ds((1 - side) * HALF, HALF)],
+                    rim_send.at[m, c, side],
+                    rim_recv.at[m, c, side],
+                    {"grid": device},
+                )
+                copy.start()
+                rim_copies[m].append(copy)
         loss_step(3 + 3 * m)
-
-        def project_rim(c, carry, m=m):
-            columns = pl.ds(pl.multiple_of(c * COLS, COLS), COLS)
-            term = dot(rim_k[...], wk[columns, :], NT) + dot(rim_v[...], wv[columns, :], NT)
-            rim_out[m, :, columns] = term.astype(BF16)
-            return carry
-
-        lax.fori_loop(0, chunks, project_rim, 0)
-        to_left = remote(
-            rim_out.at[m, pl.ds(0, HALF)],
-            rim_in.at[m, pl.ds(HALF, HALF)],
-            rim_send.at[m, 0],
-            rim_recv.at[m, 0],
-            {"grid": left},
-        )
-        to_right = remote(
-            rim_out.at[m, pl.ds(HALF, HALF)],
-            rim_in.at[m, pl.ds(0, HALF)],
-            rim_send.at[m, 1],
-            rim_recv.at[m, 1],
-            {"grid": right},
-        )
-        to_left.start()
-        to_right.start()
-        rim_copies.append((to_left, to_right))
-        loss_step(4 + 3 * m)
 
     def back_own(c, carry):
         columns = pl.ds(pl.multiple_of(c * COLS, COLS), COLS)
@@ -406,8 +441,8 @@
         )
         return carry
 
-    lax.fori_loop(0, chunks, back_own, 0)
-    for stage in range(8, len(rounds) + 1):
+    lax.fori_loop(0, chunks, back_own, 0, unroll=True)
+    for stage in range(3 * count + 1, len(rounds) + 1):
         loss_step(stage)
     loss_out[...] = loss_acc[len(rounds), 0:1, 0:1] * (1.0 / (realizations * total_points * nvars))
 
@@ -416,9 +451,10 @@
             copy.wait()
         for t in range(tiles):
             part = slice(t * HALF, (t + 1) * HALF)
-            mine = pl.ds(m * rows + t * HALF, HALF)
+            mine = place(m, t)
             normed, inverse = normalise(mem[m, part])
-            adjoint = adj_normed[mine, :] + rim_in[m, part].astype(F32)
+            rim = jnp.concatenate([rim_in[m, c, part] for c in range(chunks)], axis=1)
+            adjoint = adj_normed[mine, :] + rim.astype(F32)
             adjoint = inverse * (
                 adjoint
                 - jnp.mean(adjoint, axis=-1, keepdims=True)
@@ -444,6 +480,7 @@
     nvars = observed_truth.shape[1]
     pairs = width // LANES
     tiles = rows // HALF
+    chunks = width // COLS
     all_rows = count * rows
     stages = ens_size.bit_length() + grid_size.bit_length() - 2
     vmem = pl.BlockSpec(memory_space=pltpu.VMEM)
@@ -464,7 +501,8 @@
             pltpu.VMEM((width, width), BF16),
             pltpu.VMEM((width, width), BF16),
             pltpu.VMEM((width, width), BF16),
-            pltpu.VMEM((width, LANES), BF16),
+            pltpu.VMEM((LANES, width), BF16),
+            pltpu.VMEM((LANES, rows), F32),
             pltpu.VMEM((rows, LANES), F32),
             pltpu.VMEM((rows, LANES), F32),
             pltpu.VMEM((tiles, WINDOW, HALF), F32),
@@ -475,7 +513,8 @@
             pltpu.VMEM((count, pairs, rows + 2 * HALF, LANES), BF16),
             pltpu.VMEM((count, tiles, pairs, WINDOW, 2 * HALF), BF16),
             pltpu.VMEM((all_rows, width), BF16),
-            pltpu.VMEM((ens_size, count, rows, LANES), F32),
+            pltpu.VMEM((tiles, count * HALF, LANES), F32),
+            pltpu.VMEM((ens_size, tiles, count * HALF, LANES), BF16),
             pltpu.VMEM((all_rows, width), F32),
             pltpu.VMEM((all_rows, width), BF16),
             pltpu.VMEM((all_rows, width), BF16),
@@ -484,18 +523,18 @@
             pltpu.VMEM((all_rows, width), BF16),
             pltpu.VMEM((2 * HALF, width), BF16),
             pltpu.VMEM((2 * HALF, width), BF16),
-            pltpu.VMEM((count, 2 * HALF, width), BF16),
-            pltpu.VMEM((count, 2 * HALF, width), BF16),
+            pltpu.VMEM((count, chunks, 2 * HALF, COLS), BF16),
+            pltpu.VMEM((count, chunks, 2 * HALF, COLS), BF16),
             pltpu.VMEM((all_rows, width), F32),
             pltpu.VMEM((stages + 1, 8, LANES), F32),
             pltpu.VMEM((stages, 8, LANES), F32),
             dma((count + 4,)),
             dma((count, 2)),
             dma((count, 2)),
-            dma((ens_size - 1, count)),
-            dma((ens_size - 1, count)),
-            dma((count, 2)),
-            dma((count, 2)),
+            dma((ens_size - 1, tiles)),
+            dma((ens_size - 1, tiles)),
+            dma((count, chunks, 2)),
+            dma((count, chunks, 2)),
             dma((stages,)),
             dma((stages,)),
         ],
@@ -507,14 +546,14 @@
         ),
     )(
         members,
-        observed_truth,
+        observed_truth.T,
         cell_measure.reshape(1, rows),
         reach.reshape(1, rows),
         w_query,
         w_key,
         w_value,
         w_out,
-        readout_coefficients,
+        readout_coefficients.T,
     )
     return loss[0, 0], adjoint
 

time: 102 us -> 74.4 us (0.73)
  the two profiles are of different devices: /device:TPU:1 before, /device:TPU:32 now
where the time goes in v1:
time: 74.4 us; the launch traced here: 74.3 us
  Pallas kernels  69.7 us (94%)
  between operations  2.33 us (3%)
  local copies, waits for them, and re-layouts  2.26 us (3%)
    pallas_call x1, Pallas kernels, per_device(): pl.pallas_call(functools.partial(kernel, ens_size, grid_size, nvars), out...  69.7 us
    unnamed x1, local copies, waits for them, and re-layouts  2.26 us

profile of v1, /device:TPU:32, one launch (start us, length us, event | category | flops | bytes accessed | tf_op | source)
XLA Modules:
  0.0 74.3 jit_solution(1927787885423120019)
XLA Ops:
  0.6 69.7 %shard_map.104 = (f32[1,1]{1,0:T(1,128)}, bf16[2,256,1024]{2,1,0:T(8,128)(2,1)}) custom-call(bf16[2,256,1024]{2,1,0:T(8,128)(2,1)} %members.1, f32[100,256]{1,0:T(8,128)} %bitcast.6, f32[1,256]{1,0:T(1,128)} %bitcast.7, s32[1,256]{1,0:T(1,128)} %bitcast.8, bf16[1024,1024]{1,0:T(8,128)(2,1)} %w_query.1, bf16[1024,1024]{1,0:T(8,128)(2,1)} %w_key.1, ...), custom_call_target="tpu_custom_call" | custom-call | flops 15000000512 | bytes 12000000 | tf_op jit(solution)/shard_map/pallas_call | solution.py:489
  70.9 2.3 %copy.14 = bf16[2,256,1024]{2,1,0:T(8,128)(2,1)} copy(bf16[2,256,1024]{2,1,0:T(8,128)(2,1)} %get-tuple-element.9) | data formatting | bytes 2097152

commit v2 on v1

--- a/solution.py
+++ b/solution.py
@@ -30,8 +30,28 @@
     return lax.dot_general(a, b, dims, preferred_element_type=F32)
 
 
-def flip(index, bit):
-    return index + bit * (1 - 2 * ((index // bit) % 2))
+def flip(index, bits):
+    turned = index
+    for bit in (1 << b for b in range(bits.bit_length())):
+        if bits & bit:
+            turned = turned + bit * (1 - 2 * ((index // bit) % 2))
+    return turned
+
+
+def tree_sum(terms):
+    while len(terms) > 1:
+        terms = [terms[n] + terms[n + 1] for n in range(0, len(terms), 2)]
+    return terms[0]
+
+
+def loss_groups(ens_size, grid_size):
+    groups = [("ens", tuple(range(1, ens_size)))]
+    low = 1
+    while low < grid_size:
+        high = min(8, grid_size // low)
+        groups.append(("grid", tuple(low * n for n in range(1, high))))
+        low *= high
+    return groups
 
 
 def normalise(block):
@@ -84,16 +104,20 @@
     measure,
     bias,
     normed_own,
+    normed_wide,
+    inverse_own,
     normed_halo,
     q_s,
     k_s,
     v_s,
     p_s,
+    ds_s,
     attended,
     forecasts,
     shared,
+    folded,
+    slopes,
     adj_mixed,
-    adj_mixed_b,
     adj_attended,
     dq_s,
     dk_s,
@@ -125,10 +149,12 @@
     left = lax.rem(grid + grid_size - 1, grid_size)
     first = grid * rows
     total_points = rows * grid_size
-    ens_partners = [{"ens": flip(ens, 1)}, {"ens": flip(ens, 2)}, {"ens": flip(flip(ens, 1), 2)}]
-    ens_partners = ens_partners[: ens_size - 1]
-    rounds = [{"ens": flip(ens, 1 << b)} for b in range(ens_size.bit_length() - 1)]
-    rounds += [{"grid": flip(grid, 1 << b)} for b in range(grid_size.bit_length() - 1)]
+    ens_partners = [{"ens": flip(ens, n)} for n in range(1, ens_size)]
+    position = {"ens": ens, "grid": grid}
+    rounds = [
+        [{axis: flip(position[axis], n)} for n in numbers]
+        for axis, numbers in loss_groups(ens_size, grid_size)
+    ]
 
     def remote(source, target, send, recv, device):
         return pltpu.make_async_remote_copy(
@@ -149,7 +175,7 @@
         load.start()
 
     barrier = pltpu.get_barrier_semaphore()
-    greeted = [{"grid": left}, {"grid": right}] + ens_partners + rounds
+    greeted = [{"grid": left}, {"grid": right}] + [device for group in rounds for device in group]
     for device in greeted:
         pl.semaphore_signal(barrier, inc=1, device_id=device, device_id_type=MESH)
     pl.semaphore_wait(barrier, len(greeted))
@@ -170,9 +196,9 @@
             halo_recv.at[m, 1],
             {"grid": right},
         )
-        to_left.start()
-        to_right.start()
         halo_copies.append((to_left, to_right))
+    for copy in halo_copies[0]:
+        copy.start()
 
     adj_normed[:LANES, :] = jnp.zeros((LANES, width), F32)
     adj_normed[:nvars, :] = readout_in[...].astype(F32)
@@ -197,8 +223,14 @@
     for m in range(count):
         loads[m].wait()
         for t in range(tiles):
-            normed, _ = normalise(mem[m, t * HALF : (t + 1) * HALF])
+            normed, inverse = normalise(mem[m, t * HALF : (t + 1) * HALF])
             normed_own[place(m, t), :] = normed.astype(BF16)
+            normed_wide[place(m, t), :] = normed
+            inverse_own[place(m, t), :] = jnp.broadcast_to(inverse, (HALF, LANES))
+
+    for pair in halo_copies[1:]:
+        for copy in pair:
+            copy.start()
 
     def project_own(weight, target, start, factor, c, carry):
         columns = pl.ds(pl.multiple_of(c * COLS, COLS), COLS)
@@ -221,7 +253,6 @@
         if n:
             loads[count + n].wait()
         lax.fori_loop(0, chunks, functools.partial(project_own, *job), 0, unroll=True)
-    loads[count + 3].wait()
 
     def attend(m, some_tiles, p, carry):
         keys = k_s[m, p]
@@ -264,50 +295,52 @@
 
         lax.fori_loop(0, chunks, project_halo, 0, unroll=True)
 
-    ens_copies = []
-
-    def forecast(t):
-        these = pl.ds(t * count * HALF, count * HALF)
-
-        def mix(c, total):
-            columns = pl.ds(pl.multiple_of(c * COLS, COLS), COLS)
-            own = [mem[m, t * HALF : (t + 1) * HALF, columns] for m in range(count)]
-            mixed = dot(attended[these, :], wo[:, columns])
-            mixed = mixed + jnp.concatenate(own, axis=0).astype(F32)
-            return total + dot(mixed.astype(BF16), readout[:, columns], NT)
-
-        zero = jnp.zeros((count * HALF, LANES), F32)
-        result = lax.fori_loop(0, chunks, mix, zero, unroll=True)
-        forecasts[t] = result
-        shared[0, t] = result.astype(BF16)
+    ens_copies = [[] for _ in range(tiles)]
+
+    def fold_readout(c, carry):
+        part = pl.ds(pl.multiple_of(c * COLS, COLS), COLS)
+        folded[part, :] = dot(wo[part, :], readout[...], NT).astype(BF16)
+        return carry
+
+    def forecast(m, t):
+        these = pl.ds(m * HALF, HALF)
+        result = forecasts[t, these, :] + dot(attended[place(m, t), :], folded[...])
+        forecasts[t, these, :] = result
+        shared[0, t, m] = result.astype(BF16)
         for slot, device in enumerate(ens_partners):
             copy = remote(
-                shared.at[0, t],
-                shared.at[slot + 1, t],
-                ens_send.at[slot, t],
-                ens_recv.at[slot, t],
+                shared.at[0, t, m],
+                shared.at[slot + 1, t, m],
+                ens_send.at[slot, t, m],
+                ens_recv.at[slot, t, m],
                 device,
             )
             copy.start()
-            ens_copies.append(copy)
-
-    for m in range(count - 1):
+            ens_copies[t].append(copy)
+
+    keys_of_halo(0)
+    attend_all(0, range(tiles))
+    loads[count + 3].wait()
+    lax.fori_loop(0, chunks, fold_readout, 0, unroll=True)
+    for m in range(count):
+        base = dot(mem[m], readout[...], NT)
+        for t in range(tiles):
+            forecasts[t, m * HALF : (m + 1) * HALF, :] = base[t * HALF : (t + 1) * HALF]
+    for t in range(tiles):
+        forecast(0, t)
+    for m in range(1, count):
         keys_of_halo(m)
-        attend_all(m, range(tiles))
-    keys_of_halo(count - 1)
-    for t in range(tiles):
-        attend_all(count - 1, (t,))
-        forecast(t)
+        for t in range(tiles):
+            attend_all(m, (t,))
+            forecast(m, t)
 
     realizations = count * ens_size
     factor = 1.0 / (realizations - 1)
-    real = lax.broadcasted_iota(jnp.int32, (HALF, LANES), 1) < nvars
-
     def slopes_of(t):
         part = slice(t * HALF, (t + 1) * HALF)
         weight = measure[part, :]
         score = jnp.zeros((HALF, LANES), F32)
-        slopes = []
+        parts = []
         for m in range(count):
             mine = forecasts[t, m * HALF : (m + 1) * HALF]
             pair_sum = jnp.zeros((HALF, LANES), F32)
@@ -320,7 +353,7 @@
                     if slot == 0:
                         gap = mine - forecasts[t, theirs]
                     else:
-                        gap = mine - shared[slot, t, theirs].astype(F32)
+                        gap = mine - shared[slot, t, other].astype(F32)
                     square = gap * gap + SOFT2
                     root = lax.rsqrt(square)
                     pair_sum = pair_sum + square * root
@@ -329,75 +362,62 @@
             square = gap * gap + SOFT2
             root = lax.rsqrt(square)
             score = score + weight * (square * root - 0.5 * factor * pair_sum)
-            slopes.append((weight * (gap * root - factor * pair_slope)).astype(BF16))
-        return jnp.where(real, score, 0.0), jnp.concatenate(slopes, axis=0)
-
-    def back_to_attended(t, slopes):
+            parts.append((weight * (gap * root - factor * pair_slope)).astype(BF16))
+        return score, jnp.concatenate(parts, axis=0)
+
+    def back_to_attended(t):
+        for copy in ens_copies[t]:
+            copy.wait()
+        score, result = slopes_of(t)
         these = pl.ds(t * count * HALF, count * HALF)
-
-        def spread(c, carry):
-            columns = pl.ds(pl.multiple_of(c * COLS, COLS), COLS)
-            result = dot(slopes, readout[:, columns])
-            adj_mixed[these, columns] = result
-            adj_mixed_b[these, columns] = result.astype(BF16)
-            return carry
+        slopes[these, :] = result
 
         def back_out(c, carry):
             columns = pl.ds(pl.multiple_of(c * COLS, COLS), COLS)
-            result = dot(adj_mixed_b[these, :], wo[columns, :], NT)
-            adj_attended[these, columns] = result.astype(BF16)
+            adj_attended[these, columns] = dot(result, folded[columns, :], NT).astype(BF16)
             return carry
 
-        lax.fori_loop(0, chunks, spread, 0, unroll=True)
         lax.fori_loop(0, chunks, back_out, 0, unroll=True)
-
-    score = jnp.zeros((HALF, LANES), F32)
-    for t in range(tiles):
-        for copy in ens_copies[t * (ens_size - 1) : (t + 1) * (ens_size - 1)]:
-            copy.wait()
-        scores, slopes = slopes_of(t)
-        score = score + scores
-        back_to_attended(t, slopes)
-    loss_acc[0] = jnp.broadcast_to(jnp.sum(score, keepdims=True), (8, LANES))
+        return score
 
     pending = []
 
-    def loss_step(stage):
-        if stage > 0 and stage <= len(rounds):
-            pending[stage - 1].wait()
-            loss_acc[stage] = loss_acc[stage - 1] + loss_in[stage - 1]
-        if stage < len(rounds):
+    def loss_start(stage):
+        copies = []
+        for n, device in enumerate(rounds[stage]):
             copy = remote(
                 loss_acc.at[stage],
-                loss_in.at[stage],
-                loss_send.at[stage],
-                loss_recv.at[stage],
-                rounds[stage],
+                loss_in.at[stage, n],
+                loss_send.at[stage, n],
+                loss_recv.at[stage, n],
+                device,
             )
             copy.start()
-            pending.append(copy)
-
-    loss_step(0)
+            copies.append(copy)
+        pending.append(copies)
+
+    def loss_finish(stage):
+        for copy in pending[stage]:
+            copy.wait()
+        terms = [loss_acc[stage]] + [loss_in[stage, n] for n in range(len(rounds[stage]))]
+        loss_acc[stage + 1] = tree_sum(terms)
 
     def attend_back(m, p, carry):
         keys = k_s[m, p]
-        keys_t = keys.T
         values = v_s[m, p]
         lanes = pl.ds(pl.multiple_of(p * LANES, LANES), LANES)
         key_terms = []
         value_terms = []
         for t in range(tiles):
-            mine = place(m, t)
             window = slice(t * HALF, t * HALF + WINDOW)
             query = per_head(q_s[m, p, t * HALF : (t + 1) * HALF])
-            adjoint = per_head(adj_attended[mine, lanes])
+            adjoint = per_head(adj_attended[place(m, t), lanes])
             weights = p_s[m, t, p]
             wide = weights.astype(F32)
             adj_prob = dot(values[window], adjoint, NT)
             shift = jnp.sum(wide * adj_prob, axis=0, keepdims=True)
             adj_score = (wide * (adj_prob - shift)).astype(BF16)
-            adj_query = own_head(dot(keys_t[:, window], adj_score)) * HEAD**-0.5
-            dq_s[mine, lanes] = adj_query.astype(BF16)
+            ds_s[m, t, p] = adj_score
             key_terms.append(dot(adj_score, query) * LN2)
             value_terms.append(dot(weights, adjoint))
         for terms, own, rim in ((key_terms, dk_s, rim_k), (value_terms, dv_s, rim_v)):
@@ -409,12 +429,26 @@
                 own[place(m, t), lanes] = both[t * HALF : (t + 1) * HALF]
         return carry
 
+    def query_back(m, p, carry):
+        keys_t = k_s[m, p].T
+        lanes = pl.ds(pl.multiple_of(p * LANES, LANES), LANES)
+        for t in range(tiles):
+            window = slice(t * HALF, t * HALF + WINDOW)
+            adj_query = own_head(dot(keys_t[:, window], ds_s[m, t, p])) * HEAD**-0.5
+            dq_s[place(m, t), lanes] = adj_query.astype(BF16)
+        return carry
+
+    real = lax.broadcasted_iota(jnp.int32, (HALF, LANES), 1) < nvars
+    score = sum(back_to_attended(t) for t in range(tiles))
+    score = jnp.where(real, score, 0.0)
+    loss_acc[0] = jnp.broadcast_to(jnp.sum(score, keepdims=True), (8, LANES))
+    loss_start(0)
     rim_copies = [[] for _ in range(count)]
     for m in range(count):
-        lax.fori_loop(0, pairs // 2, functools.partial(attend_back, m), 0, unroll=True)
-        loss_step(1 + 3 * m)
-        lax.fori_loop(pairs // 2, pairs, functools.partial(attend_back, m), 0, unroll=True)
-        loss_step(2 + 3 * m)
+        lax.fori_loop(0, pairs, functools.partial(attend_back, m), 0, unroll=True)
+        if m == 1:
+            loss_finish(1)
+            loss_start(2)
 
         for c in range(chunks):
             columns = slice(c * COLS, (c + 1) * COLS)
@@ -430,8 +464,12 @@
                 )
                 copy.start()
                 rim_copies[m].append(copy)
-        loss_step(3 + 3 * m)
-
+        if m == 0:
+            loss_finish(0)
+            loss_start(1)
+
+    for m in range(count):
+        lax.fori_loop(0, pairs, functools.partial(query_back, m), 0, unroll=True)
     def back_own(c, carry):
         columns = pl.ds(pl.multiple_of(c * COLS, COLS), COLS)
         adj_normed[:, columns] = (
@@ -439,12 +477,12 @@
             + dot(dk_s[...], wk[columns, :], NT)
             + dot(dv_s[...], wv[columns, :], NT)
         )
+        adj_mixed[:, columns] = dot(slopes[...], readout[:, columns])
         return carry
 
     lax.fori_loop(0, chunks, back_own, 0, unroll=True)
-    for stage in range(3 * count + 1, len(rounds) + 1):
-        loss_step(stage)
-    loss_out[...] = loss_acc[len(rounds), 0:1, 0:1] * (1.0 / (realizations * total_points * nvars))
+    loss_finish(2)
+    loss_out[...] = loss_acc[3, 0:1, 0:1] * (1.0 / (realizations * total_points * nvars))
 
     for m in range(count):
         for copy in rim_copies[m]:
@@ -452,7 +490,8 @@
         for t in range(tiles):
             part = slice(t * HALF, (t + 1) * HALF)
             mine = place(m, t)
-            normed, inverse = normalise(mem[m, part])
+            normed = normed_wide[mine, :]
+            inverse = inverse_own[mine, :1]
             rim = jnp.concatenate([rim_in[m, c, part] for c in range(chunks)], axis=1)
             adjoint = adj_normed[mine, :] + rim.astype(F32)
             adjoint = inverse * (
@@ -482,7 +521,9 @@
     tiles = rows // HALF
     chunks = width // COLS
     all_rows = count * rows
-    stages = ens_size.bit_length() + grid_size.bit_length() - 2
+    groups = loss_groups(ens_size, grid_size)
+    stages = len(groups)
+    most = max(len(numbers) for _, numbers in groups)
     vmem = pl.BlockSpec(memory_space=pltpu.VMEM)
     anywhere = pl.BlockSpec(memory_space=pl.ANY)
     dma = pltpu.SemaphoreType.DMA
@@ -507,16 +548,20 @@
             pltpu.VMEM((rows, LANES), F32),
             pltpu.VMEM((tiles, WINDOW, HALF), F32),
             pltpu.VMEM((all_rows, width), BF16),
+            pltpu.VMEM((all_rows, width), F32),
+            pltpu.VMEM((all_rows, LANES), F32),
             pltpu.VMEM((2 * HALF, width), BF16),
             pltpu.VMEM((count, pairs, rows, LANES), BF16),
             pltpu.VMEM((count, pairs, rows + 2 * HALF, LANES), BF16),
             pltpu.VMEM((count, pairs, rows + 2 * HALF, LANES), BF16),
             pltpu.VMEM((count, tiles, pairs, WINDOW, 2 * HALF), BF16),
+            pltpu.VMEM((count, tiles, pairs, WINDOW, 2 * HALF), BF16),
             pltpu.VMEM((all_rows, width), BF16),
             pltpu.VMEM((tiles, count * HALF, LANES), F32),
-            pltpu.VMEM((ens_size, tiles, count * HALF, LANES), BF16),
+            pltpu.VMEM((ens_size, tiles, count, HALF, LANES), BF16),
+            pltpu.VMEM((width, LANES), BF16),
+            pltpu.VMEM((all_rows, LANES), BF16),
             pltpu.VMEM((all_rows, width), F32),
-            pltpu.VMEM((all_rows, width), BF16),
             pltpu.VMEM((all_rows, width), BF16),
             pltpu.VMEM((all_rows, width), BF16),
             pltpu.VMEM((all_rows, width), BF16),
@@ -527,16 +572,16 @@
             pltpu.VMEM((count, chunks, 2 * HALF, COLS), BF16),
             pltpu.VMEM((all_rows, width), F32),
             pltpu.VMEM((stages + 1, 8, LANES), F32),
-            pltpu.VMEM((stages, 8, LANES), F32),
+            pltpu.VMEM((stages, most, 8, LANES), F32),
             dma((count + 4,)),
             dma((count, 2)),
             dma((count, 2)),
-            dma((ens_size - 1, tiles)),
-            dma((ens_size - 1, tiles)),
+            dma((ens_size - 1, tiles, count)),
+            dma((ens_size - 1, tiles, count)),
             dma((count, chunks, 2)),
             dma((count, chunks, 2)),
-            dma((stages,)),
-            dma((stages,)),
+            dma((stages, most)),
+            dma((stages, most)),
         ],
         compiler_params=pltpu.CompilerParams(
             collective_id=0, has_side_effects=True, vmem_limit_bytes=60 * 1024 * 1024

time: 74.4 us -> 65.7 us (0.88)
  the two profiles are of different devices: /device:TPU:32 before, /device:TPU:1 now
where the time goes in v2:
time: 65.7 us; the launch traced here: 65.6 us
  Pallas kernels  61 us (93%)
  between operations  2.33 us (4%)
  local copies, waits for them, and re-layouts  2.26 us (3%)
    pallas_call x1, Pallas kernels, per_device(): pl.pallas_call(functools.partial(kernel, ens_size, grid_size, nvars), out...  61 us
    unnamed x1, local copies, waits for them, and re-layouts  2.26 us

profile of v2, /device:TPU:1, one launch (start us, length us, event | category | flops | bytes accessed | tf_op | source)
XLA Modules:
  0.0 65.6 jit_solution(7479966726824773251)
XLA Ops:
  0.6 61.0 %shard_map.104 = (f32[1,1]{1,0:T(1,128)}, bf16[2,256,1024]{2,1,0:T(8,128)(2,1)}) custom-call(bf16[2,256,1024]{2,1,0:T(8,128)(2,1)} %members.1, f32[100,256]{1,0:T(8,128)} %bitcast.6, f32[1,256]{1,0:T(1,128)} %bitcast.7, s32[1,256]{1,0:T(1,128)} %bitcast.8, bf16[1024,1024]{1,0:T(8,128)(2,1)} %w_query.1, bf16[1024,1024]{1,0:T(8,128)(2,1)} %w_key.1, ...), custom_call_target="tpu_custom_call" | custom-call | flops 15000000512 | bytes 12000000 | tf_op jit(solution)/shard_map/pallas_call | solution.py:530
  62.2 2.3 %copy.14 = bf16[2,256,1024]{2,1,0:T(8,128)(2,1)} copy(bf16[2,256,1024]{2,1,0:T(8,128)(2,1)} %get-tuple-element.9) | data formatting | bytes 2097152

commit v3 on v2

--- a/solution.py
+++ b/solution.py
@@ -127,9 +127,11 @@
     rim_out,
     rim_in,
     adj_normed,
+    result,
     loss_acc,
     loss_in,
     load_sem,
+    out_sem,
     halo_send,
     halo_recv,
     ens_send,
@@ -222,15 +224,14 @@
 
     for m in range(count):
         loads[m].wait()
+        if m:
+            for copy in halo_copies[m]:
+                copy.start()
         for t in range(tiles):
             normed, inverse = normalise(mem[m, t * HALF : (t + 1) * HALF])
             normed_own[place(m, t), :] = normed.astype(BF16)
             normed_wide[place(m, t), :] = normed
             inverse_own[place(m, t), :] = jnp.broadcast_to(inverse, (HALF, LANES))
-
-    for pair in halo_copies[1:]:
-        for copy in pair:
-            copy.start()
 
     def project_own(weight, target, start, factor, c, carry):
         columns = pl.ds(pl.multiple_of(c * COLS, COLS), COLS)
@@ -307,13 +308,13 @@
         result = forecasts[t, these, :] + dot(attended[place(m, t), :], folded[...])
         forecasts[t, these, :] = result
         shared[0, t, m] = result.astype(BF16)
-        for slot, device in enumerate(ens_partners):
+        for slot in reversed(range(len(ens_partners))):
             copy = remote(
                 shared.at[0, t, m],
                 shared.at[slot + 1, t, m],
                 ens_send.at[slot, t, m],
                 ens_recv.at[slot, t, m],
-                device,
+                ens_partners[slot],
             )
             copy.start()
             ens_copies[t].append(copy)
@@ -415,8 +416,11 @@
             weights = p_s[m, t, p]
             wide = weights.astype(F32)
             adj_prob = dot(values[window], adjoint, NT)
-            shift = jnp.sum(wide * adj_prob, axis=0, keepdims=True)
-            adj_score = (wide * (adj_prob - shift)).astype(BF16)
+            shift = sum(
+                jnp.sum(wide[part] * adj_prob[part], axis=0, keepdims=True)
+                for part in (slice(k, k + HALF) for k in range(0, WINDOW, HALF))
+            )
+            adj_score = weights * (adj_prob - shift).astype(BF16)
             ds_s[m, t, p] = adj_score
             key_terms.append(dot(adj_score, query) * LN2)
             value_terms.append(dot(weights, adjoint))
@@ -484,6 +488,7 @@
     loss_finish(2)
     loss_out[...] = loss_acc[3, 0:1, 0:1] * (1.0 / (realizations * total_points * nvars))
 
+    stores = []
     for m in range(count):
         for copy in rim_copies[m]:
             copy.wait()
@@ -499,7 +504,15 @@
                 - jnp.mean(adjoint, axis=-1, keepdims=True)
                 - normed * jnp.mean(adjoint * normed, axis=-1, keepdims=True)
             )
-            out[m, part] = (adj_mixed[mine, :] + adjoint).astype(BF16)
+            result[m, part] = (adj_mixed[mine, :] + adjoint).astype(BF16)
+            rows_out = pl.ds(t * HALF, HALF)
+            store = pltpu.make_async_copy(
+                result.at[m, rows_out], out.at[m, rows_out], out_sem.at[m, t]
+            )
+            store.start()
+            stores.append(store)
+    for store in stores:
+        store.wait()
 
 
 def per_device(
@@ -534,7 +547,7 @@
             jax.ShapeDtypeStruct(members.shape, BF16),
         ),
         in_specs=[anywhere, vmem, vmem, vmem, anywhere, anywhere, anywhere, anywhere, vmem],
-        out_specs=(vmem, vmem),
+        out_specs=(vmem, anywhere),
         scratch_shapes=[
             pltpu.VMEM((count, rows, width), BF16),
             pltpu.VMEM((count, 2 * HALF, width), BF16),
@@ -571,9 +584,11 @@
             pltpu.VMEM((count, chunks, 2 * HALF, COLS), BF16),
             pltpu.VMEM((count, chunks, 2 * HALF, COLS), BF16),
             pltpu.VMEM((all_rows, width), F32),
+            pltpu.VMEM((count, rows, width), BF16),
             pltpu.VMEM((stages + 1, 8, LANES), F32),
             pltpu.VMEM((stages, most, 8, LANES), F32),
             dma((count + 4,)),
+            dma((count, tiles)),
             dma((count, 2)),
             dma((count, 2)),
             dma((ens_size - 1, tiles, count)),

time: 65.7 us -> 64.4 us (0.980)
  Pallas kernels: 61 us -> 59.3 us
    pallas_call x1, Pallas kernels: 61 us -> 59.3 us  [per_device(): pl.pallas_call(functools.partial(kernel, ens_size, grid_size, nvars), out...]
where the time goes in v3:
time: 64.4 us; the launch traced here: 63.9 us
  Pallas kernels  59.3 us (92%)
  between operations  2.33 us (4%)
  local copies, waits for them, and re-layouts  2.26 us (4%)
    pallas_call x1, Pallas kernels, per_device(): pl.pallas_call(functools.partial(kernel, ens_size, grid_size, nvars), out...  59.3 us
    unnamed x1, local copies, waits for them, and re-layouts  2.26 us

profile of v3, /device:TPU:1, one launch (start us, length us, event | category | flops | bytes accessed | tf_op | source)
XLA Modules:
  0.0 63.9 jit_solution(1933930532333895540)
XLA Ops:
  0.6 59.3 %shard_map.104 = (f32[1,1]{1,0:T(1,128)}, bf16[2,256,1024]{2,1,0:T(8,128)(2,1)}) custom-call(bf16[2,256,1024]{2,1,0:T(8,128)(2,1)} %members.1, f32[100,256]{1,0:T(8,128)} %bitcast.6, f32[1,256]{1,0:T(1,128)} %bitcast.7, s32[1,256]{1,0:T(1,128)} %bitcast.8, bf16[1024,1024]{1,0:T(8,128)(2,1)} %w_query.1, bf16[1024,1024]{1,0:T(8,128)(2,1)} %w_key.1, ...), custom_call_target="tpu_custom_call" | custom-call | flops 15000000512 | bytes 12000000 | tf_op jit(solution)/shard_map/pallas_call | solution.py:543
  60.5 2.3 %copy.14 = bf16[2,256,1024]{2,1,0:T(8,128)(2,1)} copy(bf16[2,256,1024]{2,1,0:T(8,128)(2,1)} %get-tuple-element.9) | data formatting | bytes 2097152

commit v4 on v3

--- a/solution.py
+++ b/solution.py
@@ -513,6 +513,19 @@
             stores.append(store)
     for store in stores:
         store.wait()
+
+
+def hand_out(source, target, sem):
+    count, rows, _ = source.shape
+    copies = []
+    for m in range(count):
+        for t in range(rows // HALF):
+            part = pl.ds(t * HALF, HALF)
+            copy = pltpu.make_async_copy(source.at[m, part], target.at[m, part], sem.at[m, t])
+            copy.start()
+            copies.append(copy)
+    for copy in copies:
+        copy.wait()
 
 
 def per_device(
@@ -615,6 +628,13 @@
         w_out,
         readout_coefficients.T,
     )
+    adjoint = pl.pallas_call(
+        hand_out,
+        out_shape=jax.ShapeDtypeStruct(members.shape, BF16),
+        in_specs=[anywhere],
+        out_specs=anywhere,
+        scratch_shapes=[dma((count, tiles))],
+    )(adjoint)
     return loss[0, 0], adjoint
 
 

time: 64.4 us -> 95 us (1.48)
  Pallas kernels: 59.3 us -> 92.2 us
  local copies, waits for them, and re-layouts: 2.26 us -> 0 us
    pallas_call x0 -> x1, Pallas kernels: none -> 32.9 us  [per_device(): pl.pallas_call(hand_out, out_shape=jax.ShapeDtypeStruct(members.shape, BF...]
    unnamed x1 -> x0, local copies, waits for them, and re-layouts: 2.26 us -> none
where the time goes in v4:
time: 95 us; the launch traced here: 94.6 us
  Pallas kernels  92.2 us (97%)
  between operations  2.33 us (2%)
    pallas_call x1, Pallas kernels, per_device(): pl.pallas_call(functools.partial(kernel, ens_size, grid_size, nvars), out...  59.3 us
    pallas_call x1, Pallas kernels, per_device(): pl.pallas_call(hand_out, out_shape=jax.ShapeDtypeStruct(members.shape, BF...  32.9 us

profile of v4, /device:TPU:1, one launch (start us, length us, event | category | flops | bytes accessed | tf_op | source)
XLA Modules:
  0.0 94.6 jit_solution(9809283933071364534)
XLA Ops:
  0.6 59.3 %shard_map.104 = (f32[1,1]{1,0:T(1,128)}, bf16[2,256,1024]{2,1,0:T(8,128)(2,1)}) custom-call(bf16[2,256,1024]{2,1,0:T(8,128)(2,1)} %members.1, f32[100,256]{1,0:T(8,128)} %bitcast.6, f32[1,256]{1,0:T(1,128)} %bitcast.7, s32[1,256]{1,0:T(1,128)} %bitcast.8, bf16[1024,1024]{1,0:T(8,128)(2,1)} %w_query.1, bf16[1024,1024]{1,0:T(8,128)(2,1)} %w_key.1, ...), custom_call_target="tpu_custom_call" | custom-call | flops 15000000512 | bytes 12000000 | tf_op jit(solution)/shard_map/pallas_call | solution.py:556
  60.0 32.9 %shard_map.105 = bf16[2,256,1024]{2,1,0:T(8,128)(2,1)} custom-call(bf16[2,256,1024]{2,1,0:T(8,128)(2,1)} %get-tuple-element.5.source), custom_call_target="tpu_custom_call" | custom-call | tf_op jit(solution)/shard_map/pallas_call | solution.py:631
